TPU v7x, 128 devices: a whole 4x4x4 slice. The times are simulated.
128 devices in a mesh: group: 4 (over y), dev: 32 (over z, x, core).
Axes of the slice: x: 4, y: 4, z: 4, core: 2. Of those that a mesh axis runs over, the one named last changes fastest.
Arguments:
- particles: float32 [4, 16384, 128], P(None, ('group', 'dev')), may hold values from -0.95 to 0.95
- counts: int32 [16384], P(('group', 'dev')), may hold values from 1 to 128, as said below
- upward: float32 [8, 36, 36], replicated, may hold values from -0.375 to 0.375
- downward: float32 [8, 36, 36], replicated, may hold values from -0.75 to 0.75
- translate: float32 [3, 36, 36, 316], replicated, may hold values from -0.0068359375 to 0.0068359375
- far_send: int32 [128, 128, 16], P(('group', 'dev')), may hold values from -1 to 127, as said below
- mid_send: int32 [128, 128, 4], P(('group', 'dev')), may hold values from -1 to 15, as said below
- top_send: int32 [128, 4, 4], P(('group', 'dev')), may hold values from -1 to 63, as said below
- near_send: int32 [128, 128, 8], P(('group', 'dev')), may hold values from -1 to 127, as said below
- far_lists: int32 [316, 16384], P(None, ('group', 'dev')), may hold values from -1 to 2175, as said below
- mid_lists: int32 [316, 2048], P(None, ('group', 'dev')), may hold values from -1 to 527, as said below
- top_lists: int32 [316, 256], P(None, ('group', 'dev')), may hold values from -1 to 79, as said below
- near_lists: int32 [26, 16384], P(None, ('group', 'dev')), may hold values from 0 to 1151, as said below
Outputs:
- potential: float32 [16384, 128], P(('group', 'dev'))
Inputs may be any that keep to these rules, and one draw needn't show every extreme that they name: `counts`: every draw has leaves with 128 particles. `far_send`: row s, column r holds leaves of device s in its first slots and -1 after them; every device fills all 16 slots towards the next rank (wrapping) and at least half of them towards every rank. `mid_send`: as far_send, with middle-level boxes of the sender and 4 slots. `top_send`: entry (s, h, c) indexes the top-level boxes of the sender's group; filled slots come first; every device fills all 4 slots towards the next group (wrapping) and at least half of them towards every group. `near_send`: as far_send, with 8 slots. `far_lists`: slot j stands for the j-th offset of [-3, 3]^3 without [-1, 1]^3 in lexicographic order; it is -1 exactly where that offset leaves the parents' neighbourhood (floor((parity + offset) / 2) outside [-1, 1] in a coordinate, parities the bits of t mod 8 as x + 2 y + 4 z); other entries index leaf_sources of the owner and never an empty received slot. `mid_lists`: as far_lists, for middle-level boxes and mid_sources. `top_lists`: as far_lists, for top-level boxes and top_sources. `near_lists`: entries index near_sources of the owner and never an empty received slot.
All inputs are finite; a program needn't handle non-finite values.
Results may differ from a plain program's by a relative error of at most 0.0003.
Values sent between devices are 32-bit elements; how exact they have to be, the bound alone decides.
No kernel may reach another device: no remote copies, remote signals or barrier semaphores. Data moves between devices by JAX's collectives and lax.ppermute only.
A program may use at most 128 MiB of HBM per device.

v0:
```python
import math

import jax
import jax.numpy as jnp
import numpy as np
from jax import lax
from jax.experimental import pallas as pl
from jax.experimental.pallas import tpu as pltpu
from jax.sharding import PartitionSpec as P

ORDER = 6
TERMS = 36
OFFS = 316
SOFTEN = 0.01
LEAVES = 128
SLOTS = 128
RANKS = 128
AXES = ("group", "dev")
F32 = jnp.float32
BF16 = jnp.bfloat16
I32 = jnp.int32
HIGH = lax.Precision.HIGHEST
VMEM = pltpu.VMEM
SMEM = pltpu.SMEM
MIB = 1 << 20
OWN_SLOTS = 17
REST_SLOTS = 10
DUMMY = LEAVES
OWN_CLASSES = (8, 6, 4, 4)
REST_CLASSES = (11, 8, 8, 8)


def harmonics(coord_x, coord_y, coord_z):
    radius_sq = coord_x * coord_x + coord_y * coord_y + coord_z * coord_z
    real_part = {(0, 0): jnp.ones_like(coord_x)}
    imag_part = {}
    for degree in range(1, ORDER):
        scale = 1.0 / (2.0 * degree)
        if degree == 1:
            real_part[1, 1] = coord_x * scale
            imag_part[1, 1] = coord_y * scale
        else:
            prior_re = real_part[degree - 1, degree - 1]
            prior_im = imag_part[degree - 1, degree - 1]
            real_part[degree, degree] = (coord_x * prior_re - coord_y * prior_im) * scale
            imag_part[degree, degree] = (coord_x * prior_im + coord_y * prior_re) * scale
        for column in range(degree):
            factor = 1.0 / ((degree + column) * (degree - column))
            lead = ((2.0 * degree - 1.0) * factor) * coord_z
            for part in (real_part, imag_part):
                if (degree - 1, column) not in part:
                    continue
                value = lead * part[degree - 1, column]
                if column <= degree - 2:
                    value = value - (radius_sq * factor) * part[degree - 2, column]
                part[degree, column] = value
    pieces = []
    for degree in range(ORDER):
        for column in range(degree + 1):
            weight = math.sqrt(math.factorial(degree - column) * math.factorial(degree + column))
            pieces.append(weight * real_part[degree, column])
            if column > 0:
                pieces.append(weight * imag_part[degree, column])
    return pieces


def near_offsets():
    shifts = []
    for step_x in (-1, 0, 1):
        for step_y in (-1, 0, 1):
            for step_z in (-1, 0, 1):
                if step_x != 0 or step_y != 0 or step_z != 0:
                    shifts.append((step_x, step_y, step_z))
    return shifts


def far_groups():
    offsets = []
    for step_x in range(-3, 4):
        for step_y in range(-3, 4):
            for step_z in range(-3, 4):
                if max(abs(step_x), abs(step_y), abs(step_z)) >= 2:
                    offsets.append((step_x, step_y, step_z))
    groups = {}
    for j, offset in enumerate(offsets):
        mask, value = 0, 0
        for axis in range(3):
            if abs(offset[axis]) == 3:
                mask |= 1 << axis
                if offset[axis] == -3:
                    value |= 1 << axis
        key = tuple(abs(v) if abs(v) == 3 else v for v in offset)
        groups.setdefault(key, []).append((j, mask, value))
    return sorted(groups.values(), key=len)


GROUPS = far_groups()


def split3(value):
    high = value.astype(BF16).astype(F32)
    rest = value - high
    mid = rest.astype(BF16).astype(F32)
    return high, mid, rest - mid


def iota(shape, dim):
    return lax.broadcasted_iota(I32, shape, dim)


def nt(left, right):
    return lax.dot_general(left, right, (((1,), (1,)), ((), ())), precision=HIGH, preferred_element_type=F32)


def send_kernel(near_send, part, cnt, far_send, mid_send, tops, upward, sent, tab, leaf_out, mid_out, xs, table):
    filled = iota((SLOTS, LEAVES), 0) < cnt[...]
    for a in range(3):
        xs[a] = part[a].T
    xs[3] = jnp.where(filled, part[3].T, 0.0)
    comps = [part[0], part[1], part[2], xs[3].T]
    for a in range(4):
        tab[pl.ds(a, LEAVES, stride=8), :] = comps[a]
        tab[pl.ds(a + 4, LEAVES, stride=8), :] = comps[a]
    tab[8 * DUMMY : 8 * DUMMY + 8, :] = jnp.zeros((8, 128), F32)
    upper = iota((8, 128), 0) < 4

    def pack(i, carry):
        for n in range(4):
            r = i * 4 + n
            for k in range(4):
                first = jnp.maximum(near_send[r, 2 * k], 0)
                second = jnp.maximum(near_send[r, 2 * k + 1], 0)
                tile0 = tab[pl.ds(pl.multiple_of(first * 8, 8), 8), :]
                tile1 = tab[pl.ds(pl.multiple_of(second * 8, 8), 8), :]
                sent[r, 8 * k : 8 * k + 8, :] = jnp.where(upper, tile0, tile1)
        return carry

    lax.fori_loop(0, RANKS // 4, pack, 0)

    def chunk(c, acc):
        rows = pl.ds(pl.multiple_of(c * 16, 16), 16)
        charge = xs[3, rows, :]
        basis = harmonics(xs[0, rows, :], xs[1, rows, :], xs[2, rows, :])
        terms = [charge * value for value in basis]
        return tuple(old + (term[0:8] + term[8:16]) for old, term in zip(acc, terms))

    zero = jnp.zeros((8, 128), F32)
    acc = lax.fori_loop(0, SLOTS // 16, chunk, (zero,) * TERMS)
    rows = [jnp.sum(value, axis=0, keepdims=True) for value in acc]
    leaf = jnp.concatenate(rows + [jnp.zeros((4, 128), F32)], axis=0)
    leaf_out[...] = leaf
    table[...] = jnp.zeros((256, 128), F32)
    table[0:128, :] = jnp.concatenate([leaf, jnp.zeros((88, 128), F32)], axis=0).T
    mid = jnp.zeros((16, TERMS), F32)
    for o in range(8):
        mid = mid + nt(table[pl.ds(o, 16, stride=8), :][:, :TERMS], upward[o])
    table[128:144, 0:TERMS] = mid
    top = jnp.zeros((2, TERMS), F32)
    for o in range(8):
        top = top + nt(table[pl.ds(128 + o, 2, stride=8), :][:, :TERMS], upward[o])
    table[144:146, 0:TERMS] = top
    table[160:168, :] = tops[...]
    mid_wide = jnp.concatenate([table[128:144, :], jnp.zeros((112, 128), F32)], axis=0)
    mid_out[...] = mid_wide.T[0:40]
    weights = []
    for a in range(3):
        values = table[...] if a == 0 else pltpu.roll(table[...], 40 * a, 1)
        high, middle, low = split3(values)
        weights.append((jnp.concatenate([high, middle], axis=1).astype(BF16), low.astype(BF16)))
    lane = iota((128, 256), 1)

    def chosen(a, column):
        hot = jnp.where(column == lane, 1.0, 0.0).astype(BF16)
        both = jnp.dot(hot, weights[a][0], preferred_element_type=F32)
        return both[:, :128] + both[:, 128:] + jnp.dot(hot, weights[a][1], preferred_element_type=F32)

    for c in range(8):
        total = chosen(0, far_send[:, c : c + 1]) + chosen(1, far_send[:, c + 8 : c + 9])
        if c < 4:
            column = mid_send[:, c : c + 1]
            total = total + chosen(2, jnp.where(column >= 0, column + 128, -1))
        elif c < 6:
            total = total + pltpu.roll(table[140 + c : 141 + c, :], 80, 1)
        elif c == 6:
            group = lax.shift_right_logical(iota((RANKS, 128), 0), 5)
            for g in range(4):
                total = total + jnp.where(group == g, pltpu.roll(table[160 + g : 161 + g, :], 80, 1), 0.0)
        sent[:, 32 + c, :] = total


def send_pass(near_send, particles, cnt, far_send, mid_send, tops, upward):
    return pl.pallas_call(
        send_kernel,
        out_shape=(
            jax.ShapeDtypeStruct((RANKS, 40, 128), F32),
            jax.ShapeDtypeStruct(((LEAVES + 1) * 8, 128), F32),
            jax.ShapeDtypeStruct((40, 128), F32),
            jax.ShapeDtypeStruct((40, 128), F32),
        ),
        in_specs=[pl.BlockSpec(memory_space=SMEM)] + [pl.BlockSpec(memory_space=VMEM)] * 6,
        out_specs=(pl.BlockSpec(memory_space=VMEM),) * 4,
        scratch_shapes=[VMEM((4, SLOTS, LEAVES), F32), VMEM((256, 128), F32)],
        compiler_params=pltpu.CompilerParams(vmem_limit_bytes=32 * MIB),
        cost_estimate=pl.CostEstimate(flops=5_000_000, bytes_accessed=2 * MIB, transcendentals=0),
        name="send_pass",
    )(near_send, particles, cnt, far_send, mid_send, tops, upward)


def shift_tables():
    scale = np.zeros((32, 8, 128), np.float32)
    add = np.zeros((32, 8, 128), np.float32)
    shifts = near_offsets() + [(0, 0, 0)] * 6
    for j, shift in enumerate(shifts):
        for a in range(3):
            scale[j, a] = 1.0
            scale[j, a + 4] = 1.0
            add[j, a] = 2.0 * shift[a]
            add[j, a + 4] = 2.0 * shift[a]
        add[j, 3] = 1.0
    return scale.reshape(256, 128)[:8], add.reshape(256, 128)


def source_matrix(tile, scale, add, upper):
    moved = tile * scale + add
    values = jnp.where(upper, moved, moved * moved)
    high, middle, low = split3(values)
    return jnp.concatenate([high, high, middle, high, middle, low], axis=0).astype(BF16)


def build_targets(tab, target):
    upper = iota((8, 128), 0)

    def build(i, carry):
        for l in range(8):
            b = i * 8 + l
            tile = tab[pl.ds(pl.multiple_of(b * 8, 8), 8), :]
            square = jnp.where(upper < 3, tile * tile, 0.0)
            norm = jnp.sum(square, axis=0, keepdims=True) + SOFTEN
            values = jnp.where(upper < 3, -2.0 * tile, jnp.where(upper == 3, norm, jnp.where(upper < 7, 1.0, 0.0)))
            high, middle, low = split3(values)
            wide = jnp.concatenate([high, middle, high, low, middle, high], axis=0)
            target[pl.ds(pl.multiple_of(b * 128, 128), 128), :] = wide.T.astype(BF16)
        return carry

    lax.fori_loop(0, LEAVES // 8, build, 0)


def sort_leaves(counts, order, number):
    for k in range(4):
        number[k] = 0

    def collect(i, carry):
        for n in range(8):
            b = i * 8 + n
            k = lax.shift_right_logical(counts[b] - 1, 5)
            place = number[k]
            order[k * 160 + place] = b
            number[k] = place + 1
        return carry

    lax.fori_loop(0, LEAVES // 8, collect, 0)
    for k in range(4):
        for n in range(16):
            order[k * 160 + number[k] + n] = LEAVES


def near_steps(lists, tab, add_in, scale, target, field, order, number, slots, classes, own):
    upper = iota((8, 128), 0) < 4

    def source(place, shift):
        tile = tab[pl.ds(place, 8), :]
        return source_matrix(tile, scale, add_in[pl.ds(shift, 8), :], upper), tile[3:4]

    def listed(m, b):
        word = lists[m, b]
        return source(pl.multiple_of(lax.shift_right_logical(word, 5) * 8, 8), pl.multiple_of((word & 31) * 8, 8))

    def leaf_field(word, rows, start=0):
        b = jnp.minimum(word, LEAVES - 1)
        left = target[pl.ds(pl.multiple_of(b * 128, 128), rows), :]
        picked = [listed(start + m, b) for m in range(slots)]
        if own:
            picked.append(source(pl.multiple_of(b * 8, 8), 31 * 8))
        total = None
        for p in range(0, len(picked), 2):
            (mat0, charge0), (mat1, charge1) = picked[p], picked[p + 1]
            square = jnp.dot(left, jnp.concatenate([mat0, mat1], axis=1), preferred_element_type=F32)
            second = lax.rsqrt(square[:, 128:]) * charge1
            if own and p + 2 == len(picked):
                second = jnp.where(iota((rows, 128), 0) == iota((rows, 128), 1), 0.0, second)
            term = lax.rsqrt(square[:, :128]) * charge0 + second
            total = term if total is None else total + term
        value = jnp.sum(total, axis=1, keepdims=True)
        field[0:rows, :] = jnp.where(iota((rows, 128), 1) == word, field[0:rows, :] + value, field[0:rows, :])

    for k in range(4):
        rows, together = 32 * (k + 1), classes[k]
        def work(i, carry, rows=rows, together=together, k=k):
            for n in range(together):
                leaf_field(order[k * 160 + i * together + n], rows)
            return carry

        lax.fori_loop(0, (number[k] + (together - 1)) // together, work, 0)
    return leaf_field


def near_own_kernel(lists, counts, tab, scale_in, add_in, field, target, order, number):
    field[...] = jnp.zeros((SLOTS, LEAVES), F32)
    build_targets(tab, target)
    sort_leaves(counts, order, number)
    near_steps(lists, tab, add_in, scale_in[...], target, field, order, number, OWN_SLOTS, OWN_CLASSES, True)


def near_rest_kernel(lists, order, number, extra, own, received, scale_in, add_in, target, cnt, near, far, out, field, tab):
    upper = iota((8, 128), 0) < 4
    tab[0 : 8 * (LEAVES + 1), :] = own[...]

    def build(i, carry):
        for n in range(4):
            s = i * 4 + n
            for k in range(4):
                tile = received[s, 8 * k : 8 * k + 8, :]
                turned = pltpu.roll(tile, 4, 0)
                base = pl.multiple_of(8 * (LEAVES + 1) + s * 64 + k * 16, 8)
                tab[pl.ds(base, 8), :] = jnp.where(upper, tile, turned)
                tab[pl.ds(base + 8, 8), :] = jnp.where(upper, turned, tile)
        return carry

    lax.fori_loop(0, RANKS // 4, build, 0)
    field[...] = near[...] + far[...]
    leaf_field = near_steps(lists, tab, add_in, scale_in[...], target, field, order, number, REST_SLOTS, REST_CLASSES, False)

    def more(b, carry):
        def again(c, carry):
            leaf_field(b, SLOTS, c * REST_SLOTS)
            return carry

        return lax.fori_loop(1, extra[b], again, carry)

    lax.fori_loop(0, LEAVES, more, 0)
    out[...] = jnp.where(iota((SLOTS, LEAVES), 0) < cnt[...], field[...], 0.0).T


def near_own(lists, counts, tab):
    scale, add = shift_tables()
    v = pl.BlockSpec(memory_space=VMEM)
    s = pl.BlockSpec(memory_space=SMEM)
    return pl.pallas_call(
        near_own_kernel,
        out_shape=(
            jax.ShapeDtypeStruct((SLOTS, LEAVES), F32),
            jax.ShapeDtypeStruct((LEAVES * 128, 48), BF16),
            jax.ShapeDtypeStruct((640,), I32),
            jax.ShapeDtypeStruct((8,), I32),
        ),
        in_specs=[s, s] + [v] * 3,
        out_specs=(v, v, s, s),
        compiler_params=pltpu.CompilerParams(vmem_limit_bytes=32 * MIB),
        cost_estimate=pl.CostEstimate(flops=30_000_000_000, bytes_accessed=4 * MIB, transcendentals=20_000_000),
        name="near_own",
    )(lists, counts, tab, jnp.asarray(scale), jnp.asarray(add))


def near_rest(lists, order, number, extra, tab, received, target, cnt, near, far):
    scale, add = shift_tables()
    v = pl.BlockSpec(memory_space=VMEM)
    s = pl.BlockSpec(memory_space=SMEM)
    return pl.pallas_call(
        near_rest_kernel,
        out_shape=jax.ShapeDtypeStruct((LEAVES, SLOTS), F32),
        in_specs=[s, s, s, s] + [v] * 8,
        out_specs=v,
        scratch_shapes=[
            VMEM((SLOTS, LEAVES), F32),
            VMEM((8 * (LEAVES + 1 + RANKS * 8), 128), F32),
        ],
        compiler_params=pltpu.CompilerParams(vmem_limit_bytes=48 * MIB),
        cost_estimate=pl.CostEstimate(flops=10_000_000_000, bytes_accessed=8 * MIB, transcendentals=20_000_000),
        name="near_rest",
    )(lists, order, number, extra, tab, received, jnp.asarray(scale), jnp.asarray(add), target, cnt, near, far)


def near_tables(near_lists):
    own = near_lists < LEAVES
    before = jnp.cumsum(own.astype(I32), axis=0)
    slot = jnp.arange(26, dtype=I32)[:, None]
    early = own & (before <= OWN_SLOTS)
    taken = jnp.minimum(before, OWN_SLOTS)
    empty = DUMMY * 32 + 31
    word = jnp.where(own, near_lists, near_lists + 1) * 32 + slot - empty
    tables = []
    for mine, place, size in ((early, before - 1, OWN_SLOTS), (~early, slot - taken, 3 * REST_SLOTS)):
        hits = jnp.where(mine, place, -1)[None] == jnp.arange(size, dtype=I32)[:, None, None]
        tables.append(jnp.sum(jnp.where(hits, word[None], 0), axis=1) + empty)
    goes = (26 - taken[25] + (REST_SLOTS - 1)) // REST_SLOTS
    return tables[0], tables[1], goes


N1 = sum(len(g) == 1 for g in GROUPS)
N2 = sum(len(g) == 2 for g in GROUPS)
N4 = sum(len(g) == 4 for g in GROUPS)
N8 = sum(len(g) == 8 for g in GROUPS)
MERGED = len(GROUPS)
MERGED_PAD = 192


def group_words():
    words = np.zeros((MERGED_PAD, 8), np.int32)
    for m, group in enumerate(GROUPS):
        for g in range(8):
            j, mask, value = group[min(g, len(group) - 1)]
            words[m, g] = j * 64 + mask * 8 + value
    return words


def far_kernel(
    words, where_am_i, recv, leaf, mid, far_lists, small_lists, operators, downward, part,
    out, rt, merged, wide, small, xs, parents, leaves, swapped,
):
    for i in range(8):
        rt[:, 128 * i : 128 * i + 128] = recv[16 * i : 16 * i + 16, 32:40, :].reshape(128, 128).T

    def two(value):
        high = value.astype(BF16).astype(F32)
        return jnp.concatenate([high, value - high], axis=0).astype(BF16)

    table = jnp.concatenate(
        [
            two(jnp.concatenate([leaf[...], rt[0:40, :]], axis=1)),
            two(jnp.concatenate([jnp.zeros((40, 128), F32), rt[40:80, :]], axis=1)),
        ],
        axis=0,
    )
    for m, group in enumerate(GROUPS):
        row = far_lists[group[0][0] : group[0][0] + 1, :]
        for j, _, _ in group[1:]:
            row = jnp.maximum(row, far_lists[j : j + 1, :])
        merged[m : m + 1, :] = row
    merged[MERGED:, :] = jnp.full((MERGED_PAD - MERGED, 128), -1, I32)
    index = merged[...]
    rel = index - LEAVES
    slot = rel & 15
    moved = lax.shift_right_logical(slot, 3) * 8192 + LEAVES + lax.shift_right_logical(rel, 4) * 8 + (slot & 7)
    merged[...] = jnp.where(rel >= 0, moved, index)
    lane = iota((40, 128), 1)

    numbers = iota((256, 384), 0).astype(F32).astype(BF16)
    one = jnp.ones((), BF16)
    zero = jnp.zeros((), BF16)

    def hot(row, depth):
        width = row.shape[1]
        upper = lax.shift_right_arithmetic(row, 8)
        lower = (row & 255).astype(F32)
        pieces = []
        for c in range((depth + 255) // 256):
            height = min(256, depth - 256 * c)
            target = jnp.broadcast_to(jnp.where(upper == c, lower, -1.0).astype(BF16), (height, width))
            number = numbers[0:height, 0:width]
            pieces.append(jnp.where(target == number, one, zero))
        return jnp.concatenate(pieces, axis=0)

    def expand(values, m, size):
        for g in range(size):
            word = words[m, g]
            j = lax.shift_right_logical(word, 6)
            keep = (lane & (lax.shift_right_logical(word, 3) & 7)) == (word & 7)
            wide[pl.ds(j, 40, stride=320), :] = jnp.where(keep, values, 0.0)

    def block(first_row, size, together):
        def body(i, carry):
            values = []
            for n in range(together):
                m = first_row + 2 * (together * i + n)
                row = jnp.concatenate([merged[pl.ds(m, 1), :], merged[pl.ds(m + 1, 1), :]], axis=1)
                late = row >= 8192
                both = jnp.dot(table, hot(jnp.where(late, row - 8192, row), 1152), preferred_element_type=F32)
                values.append((m, jnp.where(late, both[80:120] + both[120:160], both[0:40] + both[40:80])))
            for m, value in values:
                expand(value[:, :128], m, size)
                expand(value[:, 128:], m + 1, size)
            return carry

        return body

    lax.fori_loop(0, 4, block(0, 1, 13), 0)
    lax.fori_loop(0, 4, block(N1, 2, 10), 0)
    lax.fori_loop(0, 2, block(N1 + N2, 8, 4), 0)

    def contract(left, right, dims):
        lh = left.astype(BF16)
        ll = (left - lh.astype(F32)).astype(BF16)
        rh = right.astype(BF16)
        rl = (right - rh.astype(F32)).astype(BF16)
        dot = lambda a, b: lax.dot_general(a, b, (dims, ((), ())), preferred_element_type=F32)
        return dot(lh, rh) + dot(ll, rh) + dot(lh, rl)

    for level in range(3):
        swapped[level] = pltpu.einshape("ikj->kij", operators[level])
    local = jnp.zeros((TERMS, 128), F32)
    for k in range(TERMS):
        local = local + contract(swapped[0, k], wide[320 * k : 320 * k + OFFS, :], ((1,), (0,)))

    table_small = two(jnp.concatenate([mid[...], rt[80:120, :]], axis=1))
    lists = small_lists[...]
    rel = lists - 16
    mid_place = jnp.where(rel >= 0, LEAVES + lax.shift_right_logical(rel, 2) * 8 + (rel & 3), lists)
    me = where_am_i[0]
    group = lax.shift_right_logical(me, 5)
    top_place = jnp.where(lists >= 0, LEAVES + (group * 32 + lax.shift_right_arithmetic(lists, 1)) * 8 + 4 + (lists & 1), -1)
    for h in range(4):
        row = recv[h * 32 + (me & 31), 32:40, :][6:7]
        for c in range(4):
            box = row[:, 120 + c : 121 + c].astype(I32)
            place = LEAVES + (h * 32 + lax.shift_right_arithmetic(box, 1)) * 8 + 4 + (box & 1)
            top_place = jnp.where(lists == 64 + 4 * h + c, place, top_place)
    place = jnp.where(iota(lists.shape, 0) < 16, mid_place, top_place)
    for t in range(18):
        both = jnp.dot(table_small, hot(place[t : t + 1], 1152), preferred_element_type=F32)
        value = both[0:40] + both[40:80]
        for c in range(3):
            small[c, 40 * t : 40 * t + 40, :] = value[:, 128 * c : 128 * c + 128]
    mid_local = jnp.zeros((16, TERMS), F32)
    top_local = jnp.zeros((2, TERMS), F32)

    def every_40th(start, size):
        return jnp.concatenate([small[c, pl.ds(start, size, stride=40), :] for c in range(3)], axis=1)[:, :OFFS]

    for k in range(TERMS):
        dims = ((1,), (1,))
        mid_local = mid_local + contract(every_40th(k, 16), swapped[1, k], dims)
        top_local = top_local + contract(every_40th(640 + k, 2), swapped[2, k], dims)

    for o in range(8):
        parents[pl.ds(o, 2, stride=8), 0:TERMS] = nt(top_local, downward[o])
    mid_total = parents[:, 0:TERMS] + mid_local
    leaves[...] = jnp.zeros((128, 128), F32)
    for o in range(8):
        leaves[pl.ds(o, 16, stride=8), 0:TERMS] = nt(mid_total, downward[o])
    leaves[...] = leaves[...].T
    leaves[0:TERMS, :] = leaves[0:TERMS, :] + local
    for a in range(3):
        xs[a] = part[a].T

    def chunk(c, carry):
        rows = pl.ds(pl.multiple_of(c * 16, 16), 16)
        basis = harmonics(xs[0, rows, :], xs[1, rows, :], xs[2, rows, :])
        total = leaves[0:1, :] * basis[0]
        for k in range(1, TERMS):
            total = total + leaves[k : k + 1, :] * basis[k]
        out[rows, :] = total
        return carry

    lax.fori_loop(0, SLOTS // 16, chunk, 0)


def far_pass(where_am_i, recv, leaf, mid, far_lists, small_lists, translate, downward, particles):
    v = pl.BlockSpec(memory_space=VMEM)
    s = pl.BlockSpec(memory_space=SMEM)
    return pl.pallas_call(
        far_kernel,
        out_shape=jax.ShapeDtypeStruct((SLOTS, LEAVES), F32),
        in_specs=[s, s] + [v] * 8,
        out_specs=v,
        scratch_shapes=[
            VMEM((128, 1024), F32),
            VMEM((MERGED_PAD, 128), I32),
            VMEM((40 * 320, 128), F32),
            VMEM((3, 18 * 40, 128), F32),
            VMEM((3, 128, 128), F32),
            VMEM((16, 128), F32),
            VMEM((128, 128), F32),
            VMEM((3, TERMS, TERMS, OFFS), F32),
        ],
        compiler_params=pltpu.CompilerParams(vmem_limit_bytes=48 * MIB),
        cost_estimate=pl.CostEstimate(flops=20_000_000_000, bytes_accessed=10 * MIB, transcendentals=0),
        name="far_pass",
    )(jnp.asarray(group_words()), where_am_i, recv, leaf, mid, far_lists, small_lists, translate, downward, particles)


def local(
    particles,
    counts,
    upward,
    downward,
    translate,
    far_send,
    mid_send,
    top_send,
    near_send,
    far_lists,
    mid_lists,
    top_lists,
    near_lists,
):
    me = lax.axis_index("group") * 32 + lax.axis_index("dev")
    cnt = counts.reshape(1, LEAVES)
    tops = jnp.pad(top_send[0].astype(F32), ((0, 4), (40, 84)))
    sent, tab, leaf, mid = send_pass(near_send[0], particles, cnt, far_send[0], mid_send[0], tops, upward)
    recv = lax.all_to_all(sent, AXES, split_axis=0, concat_axis=0, tiled=True)

    early, late, goes = near_tables(near_lists)
    small_lists = jnp.pad(jnp.concatenate([mid_lists, top_lists], axis=1).T, ((0, 6), (0, 68)), constant_values=-1)
    near, target, order, number = near_own(early, counts, tab)
    far = far_pass(me.reshape(1), recv, leaf, mid, far_lists, small_lists, translate, downward, particles)
    return near_rest(late, order, number, goes, tab, recv, target, cnt, near, far)


def solution(mesh):
    in_specs = (
        P(None, AXES, None),
        P(AXES),
        P(),
        P(),
        P(),
        P(AXES, None, None),
        P(AXES, None, None),
        P(AXES, None, None),
        P(AXES, None, None),
        P(None, AXES),
        P(None, AXES),
        P(None, AXES),
        P(None, AXES),
    )
    return jax.shard_map(local, mesh=mesh, in_specs=in_specs, out_specs=P(AXES, None), check_vma=False)
```

profile of v0, /device:TPU:1, one launch (start us, length us, event | category | flops | bytes accessed | tf_op | source)
XLA Modules:
  0.0 114.9 jit_solution(4451754846524449905)
XLA Ops:
  0.0 0.0 copy-start.21
  0.0 0.0 copy-start.20
  0.0 0.0 copy-start.23
  0.0 0.0 copy-start.22
  0.0 0.8 convert_bitcast_fusion
  0.8 0.8 copy.25
  1.6 0.8 copy.26
  2.4 0.8 copy.24
  3.2 0.9 copy.27.upward
  4.1 0.1 pad.8.tops
  4.2 0.9 copy-done.1
  5.2 0.7 copy-done.3
  5.8 6.5 %send_pass.1 = (f32[128,40,128]{2,1,0:T(8,128)S(1)}, f32[1032,128]{1,0:T(8,128)S(1)}, f32[40,128]{1,0:T(8,128)S(1)}, f32[40,128]{1,0:T(8,128)S(1)}) custom-call(s32[128,8]{1,0:T(8,128)S(1)} %bitcast.15, f32[4,128,128]{2,1,0:T(8,128)S(1)} %copy-done.1, s32[1,128]{1,0:T(1,128)S(1)} %bitcast.16, s32[128,16]{1,0:T(8,128)S(1)} %bitcast.13, ...), custom_call_target="tpu_custom_call" | custom-call | flops 5000000 | bytes 2097152 | tf_op jit(solution)/shard_map/send_pass/pallas_call | solution.py:192
  12.3 0.0 copy-start
  12.3 1.5 %copy-done = f32[128,40,128]{2,1,0:T(8,128)} copy-done((f32[128,40,128]{2,1,0:T(8,128)}, f32[128,40,128]{2,1,0:T(8,128)S(1)}, u32[]{:S(2)}) %copy-start) | copy-done | bytes 2621464
  13.8 0.8 copy-done.5
  14.6 11.5 %all-to-all-start = ((f32[128,40,128]{2,1,0:T(8,128)}), f32[128,40,128]{2,1,0:T(8,128)S(1)}, u32[]{:S(2)}, u32[]{:S(2)}) async-start(f32[128,40,128]{2,1,0:T(8,128)} %copy-done), calls=%async_computation | async-start | bytes 5242880 | tf_op jit(solution)/shard_map/all_to_all | solution.py:600
  26.2 0.0 copy-done.21
  26.2 0.1 select_reduce_fusion.1
  26.3 0.1 select_reduce_fusion
  26.4 0.6 bitcast_select_fusion.extra
  27.0 0.0 copy-done.20
  27.1 1.0 copy-done.6
  28.2 27.6 %near_own.1 = (f32[128,128]{1,0:T(8,128)S(1)}, bf16[16384,48]{1,0:T(8,128)(2,1)S(1)}, s32[640]{0:T(1024)S(1)}, s32[8]{0:T(128)S(1)}) custom-call(s32[17,128]{1,0:T(8,128)S(1)} %broadcast_add_fusion.1.lists, s32[128]{0:T(128)S(1)} %copy-done.4, f32[1032,128]{1,0:T(8,128)S(1)} %copy-done.6, f32[8,128]{1,0:T(8,128)S(1)} %copy-done.11, f32[256,128]{1,0:T(8,128)S(1)} %copy-done.9), custom_call_target="tpu_custom_call" | custom-call | flops 30000001024 | bytes 4194304 | tf_op jit(solution)/shard_map/near_own/pallas_call | solution.py:348
  55.8 1.9 %copy-done.13 = bf16[16384,48]{1,0:T(8,128)(2,1)} copy-done((bf16[16384,48]{1,0:T(8,128)(2,1)}, bf16[16384,48]{1,0:T(8,128)(2,1)S(1)}, u32[]{:S(2)}) %copy-start.13) | copy-done | bytes 1572888
  57.7 0.6 copy-done.14
  58.4 0.6 copy-done.16
  59.0 0.5 copy-done.18
  59.5 2.7 %all-to-all-done.recv.received = f32[128,40,128]{2,1,0:T(8,128)S(1)} async-done(((f32[128,40,128]{2,1,0:T(8,128)}), f32[128,40,128]{2,1,0:T(8,128)S(1)}, u32[]{:S(2)}, u32[]{:S(2)}) %all-to-all-start) | async-done | bytes 2621472 | tf_op jit(solution)/shard_map/all_to_all | solution.py:600
  62.3 0.0 copy-start.15
  62.3 32.2 %far_pass.1.far = f32[128,128]{1,0:T(8,128)S(1)} custom-call(s32[192,8]{1,0:T(8,128)S(1)} %copy-done.10, s32[1]{0:T(128)} %bitcast.7.where_am_i, f32[128,40,128]{2,1,0:T(8,128)S(1)} %all-to-all-done.recv.received, f32[40,128]{1,0:T(8,128)S(1)} %get-tuple-element.19.leaf, f32[40,128]{1,0:T(8,128)S(1)} %get-tuple-element.20.mid, s32[316,128]{1,0:T(8,128)S(1)} %copy-done.8, ...), custom_call_target="tpu_custom_call" | custom-call | flops 20000000000 | bytes 10485760 | tf_op jit(solution)/shard_map/far_pass/pallas_call | solution.py:560
  94.5 20.4 %near_rest.1 = f32[128,128]{1,0:T(8,128)} custom-call(s32[30,128]{1,0:T(8,128)S(1)} %broadcast_add_fusion.lists, s32[640]{0:T(1024)S(1)} %copy-done.17, s32[8]{0:T(128)S(1)} %copy-done.19, s32[128]{0:T(128)S(1)} %copy-done.12, f32[1032,128]{1,0:T(8,128)S(1)} %copy-done.7, f32[128,40,128]{2,1,0:T(8,128)S(1)} %all-to-all-done.recv.received, ...), custom_call_target="tpu_custom_call" | custom-call | flops 10000000000 | bytes 8388608 | tf_op jit(solution)/shard_map/near_rest/pallas_call | solution.py:368
  (39 shorter events, 0.2 us)
Async XLA Ops:
  0.0 27.1 %copy-start.9 = (f32[256,128]{1,0:T(8,128)S(1)}, f32[256,128]{1,0:T(8,128)}, u32[]{:S(2)}) copy-start(f32[256,128]{1,0:T(8,128)} %constant.53.clone.add_in) | copy-start | bytes 393220
  0.0 27.1 %copy-start.11 = (f32[8,128]{1,0:T(8,128)S(1)}, f32[8,128]{1,0:T(8,128)}, u32[]{:S(2)}) copy-start(f32[8,128]{1,0:T(8,128)} %constant.52.clone.scale_in) | copy-start | bytes 12292
  0.0 27.1 %copy-start.4 = (s32[128]{0:T(128)S(1)}, s32[128]{0:T(128)}, u32[]{:S(2)}) copy-start(s32[128]{0:T(128)} %counts.1) | copy-start | bytes 1540
  0.0 26.1 %copy-start.21 = (s32[26,128]{1,0:T(8,128)S(1)}, s32[26,128]{1,0:T(8,128)}, u32[]{:S(2)}) copy-start(s32[26,128]{1,0:T(8,128)} %param.30) | copy-start | bytes 39940
  0.0 27.0 %copy-start.20 = (f32[8,36,36]{2,0,1:T(8,128)S(1)}, f32[8,36,36]{2,0,1:T(8,128)}, u32[]{:S(2)}) copy-start(f32[8,36,36]{2,0,1:T(8,128)} %param.21) | copy-start | bytes 124420
  0.0 27.0 %copy-start.23 = (s32[316,2]{0,1:T(2,128)S(1)}, s32[316,2]{0,1:T(2,128)}, u32[]{:S(2)}) copy-start(s32[316,2]{0,1:T(2,128)} %param.29) | copy-start | bytes 7588
  0.0 27.0 %copy-start.22 = (s32[316,16]{0,1:T(8,128)S(1)}, s32[316,16]{0,1:T(8,128)}, u32[]{:S(2)}) copy-start(s32[316,16]{0,1:T(8,128)} %param.28) | copy-start | bytes 60676
  4.2 1.0 copy-start.1
  5.2 0.7 copy-start.3
  12.3 1.5 %copy-start = (f32[128,40,128]{2,1,0:T(8,128)}, f32[128,40,128]{2,1,0:T(8,128)S(1)}, u32[]{:S(2)}) copy-start(f32[128,40,128]{2,1,0:T(8,128)S(1)} %get-tuple-element.16) | copy-start | bytes 7864324
  13.8 0.8 copy-start.5
  14.6 47.6 %all-to-all-start = ((f32[128,40,128]{2,1,0:T(8,128)}), f32[128,40,128]{2,1,0:T(8,128)S(1)}, u32[]{:S(2)}, u32[]{:S(2)}) async-start(f32[128,40,128]{2,1,0:T(8,128)} %copy-done), calls=%async_computation | async-start | bytes 5242880 | tf_op jit(solution)/shard_map/all_to_all | solution.py:600
  27.1 1.0 copy-start.6
  28.2 34.1 %copy-start.2 = (f32[4,128,128]{2,1,0:T(8,128)S(1)}, f32[4,128,128]{2,1,0:T(8,128)}, u32[]{:S(2)}) copy-start(f32[4,128,128]{2,1,0:T(8,128)} %part.3) | copy-start | bytes 786436
  28.2 34.1 %copy-start.8 = (s32[316,128]{1,0:T(8,128)S(1)}, s32[316,128]{1,0:T(8,128)}, u32[]{:S(2)}) copy-start(s32[316,128]{1,0:T(8,128)} %far_lists.1) | copy-start | bytes 485380
  28.2 34.1 %copy-start.10 = (s32[192,8]{1,0:T(8,128)S(1)}, s32[192,8]{1,0:T(8,128)}, u32[]{:S(2)}) copy-start(s32[192,8]{1,0:T(8,128)} %constant.54.clone.words) | copy-start | bytes 18436
  55.8 1.9 %copy-start.13 = (bf16[16384,48]{1,0:T(8,128)(2,1)}, bf16[16384,48]{1,0:T(8,128)(2,1)S(1)}, u32[]{:S(2)}) copy-start(bf16[16384,48]{1,0:T(8,128)(2,1)S(1)} %get-tuple-element.17.target) | copy-start | bytes 4718596
  57.7 0.6 copy-start.14
  58.4 0.6 copy-start.16
  59.0 0.5 copy-start.18
  62.2 32.2 %copy-start.7 = (f32[1032,128]{1,0:T(8,128)S(1)}, f32[1032,128]{1,0:T(8,128)}, u32[]{:S(2)}) copy-start(f32[1032,128]{1,0:T(8,128)} %copy-done.5) | copy-start | bytes 1585156
  62.2 32.2 %copy-start.12 = (s32[128]{0:T(128)S(1)}, s32[128]{0:T(128)}, u32[]{:S(2)}) copy-start(s32[128]{0:T(128)} %bitcast_select_fusion.extra) | copy-start | bytes 1540
  62.3 32.2 %copy-start.15 = (f32[128,128]{1,0:T(8,128)S(1)}, f32[128,128]{1,0:T(8,128)}, u32[]{:S(2)}) copy-start(f32[128,128]{1,0:T(8,128)} %copy-done.14) | copy-start | bytes 196612
  62.3 32.2 %copy-start.17 = (s32[640]{0:T(1024)S(1)}, s32[640]{0:T(1024)}, u32[]{:S(2)}) copy-start(s32[640]{0:T(1024)} %copy-done.16) | copy-start | bytes 7684
  62.3 32.2 %copy-start.19 = (s32[8]{0:T(128)S(1)}, s32[8]{0:T(128)}, u32[]{:S(2)}) copy-start(s32[8]{0:T(128)} %copy-done.18) | copy-start | bytes 100
where the time goes:
time: 115 us
  Pallas kernels  86.7 us (75%)
  local copies, waits for them, and re-layouts  12.1 us (11%)
  starting transfers between devices  11.5 us (10%)
  waiting for transfers between devices  2.72 us (2%)
  other arithmetic  1.58 us (1%)
    pallas_call x1, Pallas kernels, far_pass(): pl.pallas_call(far_kernel, out_shape=jax.ShapeDtypeStruct((SLOTS, LEAVES)...  32.2 us
    pallas_call x1, Pallas kernels, near_own(): pl.pallas_call(near_own_kernel, out_shape=(jax.ShapeDtypeStruct((SLOTS, L...  27.6 us
    pallas_call x1, Pallas kernels, near_rest(): pl.pallas_call(near_rest_kernel, out_shape=jax.ShapeDtypeStruct((LEAVES,...  20.4 us
    unnamed x53, local copies, waits for them, and re-layouts  12 us
    all_to_all x1, starting transfers between devices, local(): recv = lax.all_to_all(sent, AXES, split_axis=0, concat_axis=0, tiled=True)  11.5 us
    pallas_call x1, Pallas kernels, send_pass(): pl.pallas_call(send_kernel, out_shape=(jax.ShapeDtypeStruct((RANKS, 40, 1...  6.52 us
    all_to_all x1, waiting for transfers between devices, local(): recv = lax.all_to_all(sent, AXES, split_axis=0, concat_axis=0, tiled=True)  2.72 us
  transfers between devices with their start and end apart: 1, of which 1 were waited for; matrix products, arithmetic and copies ran while one was open for 1% of the time, Pallas kernels for 24%

commit v1 on v0

--- a/solution.py
+++ b/solution.py
@@ -26,8 +26,8 @@
 OWN_SLOTS = 17
 REST_SLOTS = 10
 DUMMY = LEAVES
-OWN_CLASSES = (8, 6, 4, 4)
-REST_CLASSES = (11, 8, 8, 8)
+OWN_CLASSES = (11, 8, 6, 6)
+REST_CLASSES = (16, 11, 11, 11)
 
 
 def harmonics(coord_x, coord_y, coord_z):
@@ -112,7 +112,7 @@
     return lax.dot_general(left, right, (((1,), (1,)), ((), ())), precision=HIGH, preferred_element_type=F32)
 
 
-def send_kernel(near_send, part, cnt, far_send, mid_send, tops, upward, sent, tab, leaf_out, mid_out, xs, table):
+def send_kernel(near_send, tops, part, cnt, far_rows, mid_rows, upward_in, sent, tab, leaf_out, mid_out, xs, table):
     filled = iota((SLOTS, LEAVES), 0) < cnt[...]
     for a in range(3):
         xs[a] = part[a].T
@@ -128,8 +128,8 @@
         for n in range(4):
             r = i * 4 + n
             for k in range(4):
-                first = jnp.maximum(near_send[r, 2 * k], 0)
-                second = jnp.maximum(near_send[r, 2 * k + 1], 0)
+                first = jnp.maximum(near_send[2 * k, r], 0)
+                second = jnp.maximum(near_send[2 * k + 1, r], 0)
                 tile0 = tab[pl.ds(pl.multiple_of(first * 8, 8), 8), :]
                 tile1 = tab[pl.ds(pl.multiple_of(second * 8, 8), 8), :]
                 sent[r, 8 * k : 8 * k + 8, :] = jnp.where(upper, tile0, tile1)
@@ -151,6 +151,7 @@
     leaf_out[...] = leaf
     table[...] = jnp.zeros((256, 128), F32)
     table[0:128, :] = jnp.concatenate([leaf, jnp.zeros((88, 128), F32)], axis=0).T
+    upward = pltpu.einshape("iok->oik", upward_in[...])
     mid = jnp.zeros((16, TERMS), F32)
     for o in range(8):
         mid = mid + nt(table[pl.ds(o, 16, stride=8), :][:, :TERMS], upward[o])
@@ -159,7 +160,12 @@
     for o in range(8):
         top = top + nt(table[pl.ds(128 + o, 2, stride=8), :][:, :TERMS], upward[o])
     table[144:146, 0:TERMS] = top
-    table[160:168, :] = tops[...]
+    place = iota((1, 128), 1)
+    for g in range(4):
+        row = jnp.zeros((1, 128), F32)
+        for c in range(4):
+            row = jnp.where(place == 40 + c, tops[g, c].astype(F32), row)
+        table[160 + g : 161 + g, :] = row
     mid_wide = jnp.concatenate([table[128:144, :], jnp.zeros((112, 128), F32)], axis=0)
     mid_out[...] = mid_wide.T[0:40]
     weights = []
@@ -169,15 +175,17 @@
         weights.append((jnp.concatenate([high, middle], axis=1).astype(BF16), low.astype(BF16)))
     lane = iota((128, 256), 1)
 
+    columns = jnp.concatenate([far_rows[...], mid_rows[...], jnp.zeros((108, 128), I32)], axis=0).astype(F32).T.astype(I32)
+
     def chosen(a, column):
         hot = jnp.where(column == lane, 1.0, 0.0).astype(BF16)
         both = jnp.dot(hot, weights[a][0], preferred_element_type=F32)
         return both[:, :128] + both[:, 128:] + jnp.dot(hot, weights[a][1], preferred_element_type=F32)
 
     for c in range(8):
-        total = chosen(0, far_send[:, c : c + 1]) + chosen(1, far_send[:, c + 8 : c + 9])
+        total = chosen(0, columns[:, c : c + 1]) + chosen(1, columns[:, c + 8 : c + 9])
         if c < 4:
-            column = mid_send[:, c : c + 1]
+            column = columns[:, 16 + c : 17 + c]
             total = total + chosen(2, jnp.where(column >= 0, column + 128, -1))
         elif c < 6:
             total = total + pltpu.roll(table[140 + c : 141 + c, :], 80, 1)
@@ -188,7 +196,7 @@
         sent[:, 32 + c, :] = total
 
 
-def send_pass(near_send, particles, cnt, far_send, mid_send, tops, upward):
+def send_pass(near_send, tops, particles, cnt, far_rows, mid_rows, upward):
     return pl.pallas_call(
         send_kernel,
         out_shape=(
@@ -197,13 +205,13 @@
             jax.ShapeDtypeStruct((40, 128), F32),
             jax.ShapeDtypeStruct((40, 128), F32),
         ),
-        in_specs=[pl.BlockSpec(memory_space=SMEM)] + [pl.BlockSpec(memory_space=VMEM)] * 6,
+        in_specs=[pl.BlockSpec(memory_space=SMEM)] * 2 + [pl.BlockSpec(memory_space=VMEM)] * 5,
         out_specs=(pl.BlockSpec(memory_space=VMEM),) * 4,
         scratch_shapes=[VMEM((4, SLOTS, LEAVES), F32), VMEM((256, 128), F32)],
-        compiler_params=pltpu.CompilerParams(vmem_limit_bytes=32 * MIB),
+        compiler_params=pltpu.CompilerParams(vmem_limit_bytes=63 * MIB),
         cost_estimate=pl.CostEstimate(flops=5_000_000, bytes_accessed=2 * MIB, transcendentals=0),
         name="send_pass",
-    )(near_send, particles, cnt, far_send, mid_send, tops, upward)
+    )(near_send, tops, particles, cnt, far_rows, mid_rows, upward)
 
 
 def shift_tables():
@@ -355,7 +363,7 @@
         ),
         in_specs=[s, s] + [v] * 3,
         out_specs=(v, v, s, s),
-        compiler_params=pltpu.CompilerParams(vmem_limit_bytes=32 * MIB),
+        compiler_params=pltpu.CompilerParams(vmem_limit_bytes=63 * MIB),
         cost_estimate=pl.CostEstimate(flops=30_000_000_000, bytes_accessed=4 * MIB, transcendentals=20_000_000),
         name="near_own",
     )(lists, counts, tab, jnp.asarray(scale), jnp.asarray(add))
@@ -374,7 +382,7 @@
             VMEM((SLOTS, LEAVES), F32),
             VMEM((8 * (LEAVES + 1 + RANKS * 8), 128), F32),
         ],
-        compiler_params=pltpu.CompilerParams(vmem_limit_bytes=48 * MIB),
+        compiler_params=pltpu.CompilerParams(vmem_limit_bytes=63 * MIB),
         cost_estimate=pl.CostEstimate(flops=10_000_000_000, bytes_accessed=8 * MIB, transcendentals=20_000_000),
         name="near_rest",
     )(lists, order, number, extra, tab, received, jnp.asarray(scale), jnp.asarray(add), target, cnt, near, far)
@@ -414,7 +422,7 @@
 
 
 def far_kernel(
-    words, where_am_i, recv, leaf, mid, far_lists, small_lists, operators, downward, part,
+    words, where_am_i, recv, leaf, mid, far_lists, small_lists, operators, downward_in, part,
     out, rt, merged, wide, small, xs, parents, leaves, swapped,
 ):
     for i in range(8):
@@ -531,6 +539,7 @@
         mid_local = mid_local + contract(every_40th(k, 16), swapped[1, k], dims)
         top_local = top_local + contract(every_40th(640 + k, 2), swapped[2, k], dims)
 
+    downward = pltpu.einshape("iok->oik", downward_in[...])
     for o in range(8):
         parents[pl.ds(o, 2, stride=8), 0:TERMS] = nt(top_local, downward[o])
     mid_total = parents[:, 0:TERMS] + mid_local
@@ -572,7 +581,7 @@
             VMEM((128, 128), F32),
             VMEM((3, TERMS, TERMS, OFFS), F32),
         ],
-        compiler_params=pltpu.CompilerParams(vmem_limit_bytes=48 * MIB),
+        compiler_params=pltpu.CompilerParams(vmem_limit_bytes=63 * MIB),
         cost_estimate=pl.CostEstimate(flops=20_000_000_000, bytes_accessed=10 * MIB, transcendentals=0),
         name="far_pass",
     )(jnp.asarray(group_words()), where_am_i, recv, leaf, mid, far_lists, small_lists, translate, downward, particles)
@@ -595,14 +604,15 @@
 ):
     me = lax.axis_index("group") * 32 + lax.axis_index("dev")
     cnt = counts.reshape(1, LEAVES)
-    tops = jnp.pad(top_send[0].astype(F32), ((0, 4), (40, 84)))
-    sent, tab, leaf, mid = send_pass(near_send[0], particles, cnt, far_send[0], mid_send[0], tops, upward)
+    sent, tab, leaf, mid = send_pass(
+        near_send[0].T, top_send[0], particles, cnt, far_send[0].T, mid_send[0].T, upward.transpose(1, 0, 2)
+    )
     recv = lax.all_to_all(sent, AXES, split_axis=0, concat_axis=0, tiled=True)
 
     early, late, goes = near_tables(near_lists)
     small_lists = jnp.pad(jnp.concatenate([mid_lists, top_lists], axis=1).T, ((0, 6), (0, 68)), constant_values=-1)
     near, target, order, number = near_own(early, counts, tab)
-    far = far_pass(me.reshape(1), recv, leaf, mid, far_lists, small_lists, translate, downward, particles)
+    far = far_pass(me.reshape(1), recv, leaf, mid, far_lists, small_lists, translate, downward.transpose(1, 0, 2), particles)
     return near_rest(late, order, number, goes, tab, recv, target, cnt, near, far)
 
 

time: 115 us -> 110 us (0.957); the launches traced: 115 us -> 108 us
  local copies, waits for them, and re-layouts: 12.1 us -> 0.63 us
  waiting for transfers between devices: 2.72 us -> 6.87 us
    unnamed x53 -> x6, local copies, waits for them, and re-layouts: 12 us -> 0.01 us
    all_to_all x1, waiting for transfers between devices: 2.72 us -> 6.87 us  [local(): recv = lax.all_to_all(sent, AXES, split_axis=0, concat_axis=0, tiled=True)]
    pallas_call x1, Pallas kernels: 6.52 us -> 7.97 us  [send_pass(): pl.pallas_call(send_kernel, out_shape=(jax.ShapeDtypeStruct((RANKS, 40, 1...]
    pallas_call x1, Pallas kernels: 32.2 us -> 33.6 us  [far_pass(): pl.pallas_call(far_kernel, out_shape=jax.ShapeDtypeStruct((SLOTS, LEAVES)...]
    pallas_call x1, Pallas kernels: 27.6 us -> 26.2 us  [near_own(): pl.pallas_call(near_own_kernel, out_shape=(jax.ShapeDtypeStruct((SLOTS, L...]
    pallas_call x1, Pallas kernels: 20.4 us -> 19.2 us  [near_rest(): pl.pallas_call(near_rest_kernel, out_shape=jax.ShapeDtypeStruct((LEAVES,...]
    add x2, other arithmetic: 0.01 us -> 1.21 us  [near_tables(): tables.append(jnp.sum(jnp.where(hits, word[None], 0), axis=1) + empty)]
  transfers between devices with their start and end apart: 1 -> 1, of which waited for: 1 -> 1; matrix products, arithmetic and copies ran while one was open for 1% -> 2% of each run, Pallas kernels for 24% -> 24%
where the time goes in v1:
time: 110 us; the launch traced here: 108 us
  Pallas kernels  87 us (79%)
  starting transfers between devices  11.9 us (11%)
  waiting for transfers between devices  6.87 us (6%)
  other arithmetic  2 us (2%)
    pallas_call x1, Pallas kernels, far_pass(): pl.pallas_call(far_kernel, out_shape=jax.ShapeDtypeStruct((SLOTS, LEAVES)...  33.6 us
    pallas_call x1, Pallas kernels, near_own(): pl.pallas_call(near_own_kernel, out_shape=(jax.ShapeDtypeStruct((SLOTS, L...  26.2 us
    pallas_call x1, Pallas kernels, near_rest(): pl.pallas_call(near_rest_kernel, out_shape=jax.ShapeDtypeStruct((LEAVES,...  19.2 us
    all_to_all x1, starting transfers between devices, local(): recv = lax.all_to_all(sent, AXES, split_axis=0, concat_axis=0, tiled=True)  11.9 us
    pallas_call x1, Pallas kernels, send_pass(): pl.pallas_call(send_kernel, out_shape=(jax.ShapeDtypeStruct((RANKS, 40, 1...  7.97 us
    all_to_all x1, waiting for transfers between devices, local(): recv = lax.all_to_all(sent, AXES, split_axis=0, concat_axis=0, tiled=True)  6.87 us
  transfers between devices with their start and end apart: 1, of which 1 were waited for; matrix products, arithmetic and copies ran while one was open for 2% of the time, Pallas kernels for 24%

profile of v1, /device:TPU:1, one launch (start us, length us, event | category | flops | bytes accessed | tf_op | source)
XLA Modules:
  0.0 108.4 jit_solution(14399582454737803673)
XLA Ops:
  0.0 0.0 copy-start
  0.0 0.0 copy-start.2
  0.0 0.0 copy-start.1
  0.0 8.0 %send_pass.1 = (f32[128,40,128]{2,1,0:T(8,128)}, f32[1032,128]{1,0:T(8,128)}, f32[40,128]{1,0:T(8,128)}, f32[40,128]{1,0:T(8,128)}) custom-call(s32[8,128]{1,0:T(8,128)} %bitcast.22, s32[4,4]{1,0:T(4,128)} %bitcast.23, f32[4,128,128]{2,1,0:T(8,128)} %part.3, s32[1,128]{1,0:T(1,128)} %bitcast.25, s32[16,128]{1,0:T(8,128)} %bitcast.21, s32[4,128]{1,0:T(4,128)} %bitcast.24, ...), custom_call_target="tpu_custom_call" | custom-call | flops 5000000 | bytes 2097152 | tf_op jit(solution)/shard_map/send_pass/pallas_call | solution.py:200
  8.0 11.9 %all-to-all-start = ((f32[128,40,128]{2,1,0:T(8,128)}), f32[128,40,128]{2,1,0:T(8,128)}, u32[]{:S(2)}, u32[]{:S(2)}) async-start(f32[128,40,128]{2,1,0:T(8,128)} %get-tuple-element.16), calls=%async_computation | async-start | bytes 5242880 | tf_op jit(solution)/shard_map/all_to_all | solution.py:610
  19.9 0.0 copy-done
  20.0 0.1 select_reduce_fusion.1
  20.0 0.1 select_reduce_fusion
  20.1 0.6 broadcast_add_fusion.lists
  20.7 0.6 broadcast_add_fusion.1.lists
  21.3 0.6 bitcast_select_fusion.extra
  21.9 0.0 copy-done.2
  21.9 0.0 copy-done.1
  21.9 0.6 pad.4.small_lists
  22.6 26.2 %near_own.1 = (f32[128,128]{1,0:T(8,128)}, bf16[16384,48]{1,0:T(8,128)(2,1)}, s32[640]{0:T(1024)}, s32[8]{0:T(128)}) custom-call(s32[17,128]{1,0:T(8,128)} %broadcast_add_fusion.1.lists, s32[128]{0:T(128)} %counts.1, f32[1032,128]{1,0:T(8,128)} %get-tuple-element.13.tab.own, f32[8,128]{1,0:T(8,128)} %constant.50.clone.scale_in, f32[256,128]{1,0:T(8,128)} %constant.51.clone.add_in), custom_call_target="tpu_custom_call" | custom-call | flops 30000001024 | bytes 4194304 | tf_op jit(solution)/shard_map/near_own/pallas_call | solution.py:356
  48.8 6.9 %all-to-all-done.recv.received = f32[128,40,128]{2,1,0:T(8,128)} async-done(((f32[128,40,128]{2,1,0:T(8,128)}), f32[128,40,128]{2,1,0:T(8,128)}, u32[]{:S(2)}, u32[]{:S(2)}) %all-to-all-start) | async-done | bytes 2621472 | tf_op jit(solution)/shard_map/all_to_all | solution.py:610
  55.7 33.6 %far_pass.1.far = f32[128,128]{1,0:T(8,128)} custom-call(s32[192,8]{1,0:T(8,128)} %constant.52.clone.words, s32[1]{0:T(128)} %bitcast.11.where_am_i, f32[128,40,128]{2,1,0:T(8,128)} %all-to-all-done.recv.received, f32[40,128]{1,0:T(8,128)} %get-tuple-element.19.leaf, f32[40,128]{1,0:T(8,128)} %get-tuple-element.20.mid, s32[316,128]{1,0:T(8,128)} %far_lists.1, ...), custom_call_target="tpu_custom_call" | custom-call | flops 20000000000 | bytes 10485760 | tf_op jit(solution)/shard_map/far_pass/pallas_call | solution.py:569
  89.3 19.2 %near_rest.1 = f32[128,128]{1,0:T(8,128)} custom-call(s32[30,128]{1,0:T(8,128)} %broadcast_add_fusion.lists, s32[640]{0:T(1024)} %get-tuple-element.14.order, s32[8]{0:T(128)} %get-tuple-element.15.number, s32[128]{0:T(128)} %bitcast_select_fusion.extra, f32[1032,128]{1,0:T(8,128)} %get-tuple-element.13.tab.own, f32[128,40,128]{2,1,0:T(8,128)} %all-to-all-done.recv.received, ...), custom_call_target="tpu_custom_call" | custom-call | flops 10000000000 | bytes 8388608 | tf_op jit(solution)/shard_map/near_rest/pallas_call | solution.py:376
  (4 shorter events, 0.1 us)
Async XLA Ops:
  0.0 19.9 %copy-start = (s32[26,128]{1,0:T(8,128)S(1)}, s32[26,128]{1,0:T(8,128)}, u32[]{:S(2)}) copy-start(s32[26,128]{1,0:T(8,128)} %param.30) | copy-start | bytes 39940
  0.0 21.9 %copy-start.2 = (s32[316,2]{0,1:T(2,128)S(1)}, s32[316,2]{0,1:T(2,128)}, u32[]{:S(2)}) copy-start(s32[316,2]{0,1:T(2,128)} %param.29) | copy-start | bytes 7588
  0.0 21.9 %copy-start.1 = (s32[316,16]{0,1:T(8,128)S(1)}, s32[316,16]{0,1:T(8,128)}, u32[]{:S(2)}) copy-start(s32[316,16]{0,1:T(8,128)} %param.28) | copy-start | bytes 60676
  8.0 47.7 %all-to-all-start = ((f32[128,40,128]{2,1,0:T(8,128)}), f32[128,40,128]{2,1,0:T(8,128)}, u32[]{:S(2)}, u32[]{:S(2)}) async-start(f32[128,40,128]{2,1,0:T(8,128)} %get-tuple-element.16), calls=%async_computation | async-start | bytes 5242880 | tf_op jit(solution)/shard_map/all_to_all | solution.py:610

commit v2 on v1

--- a/solution.py
+++ b/solution.py
@@ -319,8 +319,10 @@
     near_steps(lists, tab, add_in, scale_in[...], target, field, order, number, OWN_SLOTS, OWN_CLASSES, True)
 
 
-def near_rest_kernel(lists, order, number, extra, own, received, scale_in, add_in, target, cnt, near, far, out, field, tab):
+def near_rest_kernel(lists, order, number, extra, own, received, scale_in, add_in, target_in, cnt, near, far, out, field, tab, target, arrived):
     upper = iota((8, 128), 0) < 4
+    fetch = pltpu.make_async_copy(target_in, target, arrived)
+    fetch.start()
     tab[0 : 8 * (LEAVES + 1), :] = own[...]
 
     def build(i, carry):
@@ -336,6 +338,7 @@
 
     lax.fori_loop(0, RANKS // 4, build, 0)
     field[...] = near[...] + far[...]
+    fetch.wait()
     leaf_field = near_steps(lists, tab, add_in, scale_in[...], target, field, order, number, REST_SLOTS, REST_CLASSES, False)
 
     def more(b, carry):
@@ -376,11 +379,13 @@
     return pl.pallas_call(
         near_rest_kernel,
         out_shape=jax.ShapeDtypeStruct((LEAVES, SLOTS), F32),
-        in_specs=[s, s, s, s] + [v] * 8,
+        in_specs=[s, s, s, s] + [v] * 4 + [pl.BlockSpec(memory_space=pl.ANY)] + [v] * 3,
         out_specs=v,
         scratch_shapes=[
             VMEM((SLOTS, LEAVES), F32),
             VMEM((8 * (LEAVES + 1 + RANKS * 8), 128), F32),
+            VMEM((LEAVES * 128, 48), BF16),
+            pltpu.SemaphoreType.DMA,
         ],
         compiler_params=pltpu.CompilerParams(vmem_limit_bytes=63 * MIB),
         cost_estimate=pl.CostEstimate(flops=10_000_000_000, bytes_accessed=8 * MIB, transcendentals=20_000_000),
@@ -410,6 +415,7 @@
 N8 = sum(len(g) == 8 for g in GROUPS)
 MERGED = len(GROUPS)
 MERGED_PAD = 192
+WIDE = 321
 
 
 def group_words():
@@ -422,9 +428,11 @@
 
 
 def far_kernel(
-    words, where_am_i, recv, leaf, mid, far_lists, small_lists, operators, downward_in, part,
-    out, rt, merged, wide, small, xs, parents, leaves, swapped,
+    words, where_am_i, recv, leaf, mid, far_lists, small_lists, operators_in, downward_in, part,
+    out, rt, merged, wide, small, xs, parents, leaves, swapped, operators, arrived,
 ):
+    fetch = pltpu.make_async_copy(operators_in, operators, arrived)
+    fetch.start()
     for i in range(8):
         rt[:, 128 * i : 128 * i + 128] = recv[16 * i : 16 * i + 16, 32:40, :].reshape(128, 128).T
 
@@ -473,7 +481,7 @@
             word = words[m, g]
             j = lax.shift_right_logical(word, 6)
             keep = (lane & (lax.shift_right_logical(word, 3) & 7)) == (word & 7)
-            wide[pl.ds(j, 40, stride=320), :] = jnp.where(keep, values, 0.0)
+            wide[pl.ds(j, 40, stride=WIDE), :] = jnp.where(keep, values, 0.0)
 
     def block(first_row, size, together):
         def body(i, carry):
@@ -503,11 +511,12 @@
         dot = lambda a, b: lax.dot_general(a, b, (dims, ((), ())), preferred_element_type=F32)
         return dot(lh, rh) + dot(ll, rh) + dot(lh, rl)
 
+    fetch.wait()
     for level in range(3):
         swapped[level] = pltpu.einshape("ikj->kij", operators[level])
     local = jnp.zeros((TERMS, 128), F32)
     for k in range(TERMS):
-        local = local + contract(swapped[0, k], wide[320 * k : 320 * k + OFFS, :], ((1,), (0,)))
+        local = local + contract(swapped[0, k], wide[WIDE * k : WIDE * k + OFFS, :], ((1,), (0,)))
 
     table_small = two(jnp.concatenate([mid[...], rt[80:120, :]], axis=1))
     lists = small_lists[...]
@@ -569,17 +578,19 @@
     return pl.pallas_call(
         far_kernel,
         out_shape=jax.ShapeDtypeStruct((SLOTS, LEAVES), F32),
-        in_specs=[s, s] + [v] * 8,
+        in_specs=[s, s] + [v] * 5 + [pl.BlockSpec(memory_space=pl.ANY)] + [v] * 2,
         out_specs=v,
         scratch_shapes=[
             VMEM((128, 1024), F32),
             VMEM((MERGED_PAD, 128), I32),
-            VMEM((40 * 320, 128), F32),
+            VMEM((40 * WIDE, 128), F32),
             VMEM((3, 18 * 40, 128), F32),
             VMEM((3, 128, 128), F32),
             VMEM((16, 128), F32),
             VMEM((128, 128), F32),
             VMEM((3, TERMS, TERMS, OFFS), F32),
+            VMEM((3, TERMS, TERMS, OFFS), F32),
+            pltpu.SemaphoreType.DMA,
         ],
         compiler_params=pltpu.CompilerParams(vmem_limit_bytes=63 * MIB),
         cost_estimate=pl.CostEstimate(flops=20_000_000_000, bytes_accessed=10 * MIB, transcendentals=0),

time: 110 us -> 102 us (0.927); the launches traced: 108 us -> 102 us
  Pallas kernels: 87 us -> 81.7 us
    pallas_call x1, Pallas kernels: 33.6 us -> 25 us  [far_pass(): pl.pallas_call(far_kernel, out_shape=jax.ShapeDtypeStruct((SLOTS, LEAVES)...]
    pallas_call x1, Pallas kernels: 19.2 us -> 21.4 us  [near_rest(): pl.pallas_call(near_rest_kernel, out_shape=jax.ShapeDtypeStruct((LEAVES,...]
  transfers between devices with their start and end apart: 1 -> 1, of which waited for: 1 -> 1; matrix products, arithmetic and copies ran while one was open for 2% -> 3% of each run, Pallas kernels for 24% -> 27%
where the time goes in v2:
time: 102 us
  Pallas kernels  81.7 us (80%)
  starting transfers between devices  11.9 us (12%)
  waiting for transfers between devices  5.78 us (6%)
  other arithmetic  2 us (2%)
    pallas_call x1, Pallas kernels, near_own(): pl.pallas_call(near_own_kernel, out_shape=(jax.ShapeDtypeStruct((SLOTS, L...  27.3 us
    pallas_call x1, Pallas kernels, far_pass(): pl.pallas_call(far_kernel, out_shape=jax.ShapeDtypeStruct((SLOTS, LEAVES)...  25 us
    pallas_call x1, Pallas kernels, near_rest(): pl.pallas_call(near_rest_kernel, out_shape=jax.ShapeDtypeStruct((LEAVES,...  21.4 us
    all_to_all x1, starting transfers between devices, local(): recv = lax.all_to_all(sent, AXES, split_axis=0, concat_axis=0, tiled=True)  11.9 us
    pallas_call x1, Pallas kernels, send_pass(): pl.pallas_call(send_kernel, out_shape=(jax.ShapeDtypeStruct((RANKS, 40, 1...  7.97 us
    all_to_all x1, waiting for transfers between devices, local(): recv = lax.all_to_all(sent, AXES, split_axis=0, concat_axis=0, tiled=True)  5.78 us
  transfers between devices with their start and end apart: 1, of which 1 were waited for; matrix products, arithmetic and copies ran while one was open for 3% of the time, Pallas kernels for 27%

profile of v2, /device:TPU:1, one launch (start us, length us, event | category | flops | bytes accessed | tf_op | source)
XLA Modules:
  0.0 102.3 jit_solution(12983347856076553859)
XLA Ops:
  0.0 0.0 copy-start
  0.0 0.0 copy-start.2
  0.0 0.0 copy-start.1
  0.0 8.0 %send_pass.1 = (f32[128,40,128]{2,1,0:T(8,128)}, f32[1032,128]{1,0:T(8,128)}, f32[40,128]{1,0:T(8,128)}, f32[40,128]{1,0:T(8,128)}) custom-call(s32[8,128]{1,0:T(8,128)} %bitcast.22, s32[4,4]{1,0:T(4,128)} %bitcast.23, f32[4,128,128]{2,1,0:T(8,128)} %part.3, s32[1,128]{1,0:T(1,128)} %bitcast.25, s32[16,128]{1,0:T(8,128)} %bitcast.21, s32[4,128]{1,0:T(4,128)} %bitcast.24, ...), custom_call_target="tpu_custom_call" | custom-call | flops 5000000 | bytes 2097152 | tf_op jit(solution)/shard_map/send_pass/pallas_call | solution.py:200
  8.0 11.9 %all-to-all-start = ((f32[128,40,128]{2,1,0:T(8,128)}), f32[128,40,128]{2,1,0:T(8,128)}, u32[]{:S(2)}, u32[]{:S(2)}) async-start(f32[128,40,128]{2,1,0:T(8,128)} %get-tuple-element.16), calls=%async_computation | async-start | bytes 5242880 | tf_op jit(solution)/shard_map/all_to_all | solution.py:621
  19.9 0.0 copy-done
  20.0 0.1 select_reduce_fusion.1
  20.0 0.1 select_reduce_fusion
  20.1 0.6 broadcast_add_fusion.lists
  20.7 0.6 broadcast_add_fusion.1.lists
  21.3 0.6 bitcast_select_fusion.extra
  21.9 0.0 copy-done.2
  21.9 0.0 copy-done.1
  21.9 0.6 pad.4.small_lists
  22.6 27.3 %near_own.1 = (f32[128,128]{1,0:T(8,128)}, bf16[16384,48]{1,0:T(8,128)(2,1)}, s32[640]{0:T(1024)}, s32[8]{0:T(128)}) custom-call(s32[17,128]{1,0:T(8,128)} %broadcast_add_fusion.1.lists, s32[128]{0:T(128)} %counts.1, f32[1032,128]{1,0:T(8,128)} %get-tuple-element.13.tab.own, f32[8,128]{1,0:T(8,128)} %constant.50.clone.scale_in, f32[256,128]{1,0:T(8,128)} %constant.51.clone.add_in), custom_call_target="tpu_custom_call" | custom-call | flops 30000001024 | bytes 4194304 | tf_op jit(solution)/shard_map/near_own/pallas_call | solution.py:359
  49.9 5.8 %all-to-all-done.recv.received = f32[128,40,128]{2,1,0:T(8,128)} async-done(((f32[128,40,128]{2,1,0:T(8,128)}), f32[128,40,128]{2,1,0:T(8,128)}, u32[]{:S(2)}, u32[]{:S(2)}) %all-to-all-start) | async-done | bytes 2621472 | tf_op jit(solution)/shard_map/all_to_all | solution.py:621
  55.7 25.0 %far_pass.1.far = f32[128,128]{1,0:T(8,128)} custom-call(s32[192,8]{1,0:T(8,128)} %constant.52.clone.words, s32[1]{0:T(128)} %bitcast.11.where_am_i, f32[128,40,128]{2,1,0:T(8,128)} %all-to-all-done.recv.received, f32[40,128]{1,0:T(8,128)} %get-tuple-element.19.leaf, f32[40,128]{1,0:T(8,128)} %get-tuple-element.20.mid, s32[316,128]{1,0:T(8,128)} %far_lists.1, ...), custom_call_target="tpu_custom_call" | custom-call | flops 20000000000 | bytes 10485760 | tf_op jit(solution)/shard_map/far_pass/pallas_call | solution.py:578
  80.7 21.4 %near_rest.1 = f32[128,128]{1,0:T(8,128)} custom-call(s32[30,128]{1,0:T(8,128)} %broadcast_add_fusion.lists, s32[640]{0:T(1024)} %get-tuple-element.14.order, s32[8]{0:T(128)} %get-tuple-element.15.number, s32[128]{0:T(128)} %bitcast_select_fusion.extra, f32[1032,128]{1,0:T(8,128)} %get-tuple-element.13.tab.own, f32[128,40,128]{2,1,0:T(8,128)} %all-to-all-done.recv.received, ...), custom_call_target="tpu_custom_call" | custom-call | flops 10000000000 | bytes 8388608 | tf_op jit(solution)/shard_map/near_rest/pallas_call | solution.py:379
  (4 shorter events, 0.1 us)
Async XLA Ops:
  0.0 19.9 %copy-start = (s32[26,128]{1,0:T(8,128)S(1)}, s32[26,128]{1,0:T(8,128)}, u32[]{:S(2)}) copy-start(s32[26,128]{1,0:T(8,128)} %param.30) | copy-start | bytes 39940
  0.0 21.9 %copy-start.2 = (s32[316,2]{0,1:T(2,128)S(1)}, s32[316,2]{0,1:T(2,128)}, u32[]{:S(2)}) copy-start(s32[316,2]{0,1:T(2,128)} %param.29) | copy-start | bytes 7588
  0.0 21.9 %copy-start.1 = (s32[316,16]{0,1:T(8,128)S(1)}, s32[316,16]{0,1:T(8,128)}, u32[]{:S(2)}) copy-start(s32[316,16]{0,1:T(8,128)} %param.28) | copy-start | bytes 60676
  8.0 47.7 %all-to-all-start = ((f32[128,40,128]{2,1,0:T(8,128)}), f32[128,40,128]{2,1,0:T(8,128)}, u32[]{:S(2)}, u32[]{:S(2)}) async-start(f32[128,40,128]{2,1,0:T(8,128)} %get-tuple-element.16), calls=%async_computation | async-start | bytes 5242880 | tf_op jit(solution)/shard_map/all_to_all | solution.py:621
